TPU v7x, 32 devices: a whole 2x2x4 slice. The times are simulated.
32 devices in a mesh: row: 8 (over z, core), col: 4 (over y, x).
Axes of the slice: x: 2, y: 2, z: 4, core: 2. Of those that a mesh axis runs over, the one named last changes fastest.
Arguments:
- out_grad: bfloat16 [16384, 256], P(('row', 'col')), may hold values from -6 to 6
- out_bits: int32 [16384, 16], P(('row', 'col')), may hold values from 0 to 65535
- agg_saved: bfloat16 [16384, 256], P(('row', 'col')), may hold values from -6 to 6
- weight: bfloat16 [256, 256], replicated, may hold values from -0.375 to 0.375
- tiles: bfloat16 [8, 4, 512, 128, 128], P('row', 'col'), may hold values from -0.0625 to 0.0625
- tile_coords: int32 [8, 4, 512, 2], P('row', 'col'), may hold values from 0 to 31, as said below
- tile_count: int32 [8, 4], P('row', 'col'), may hold values from 64 to 512, as said below
- in_bits: int32 [16384, 16], P(('row', 'col')), may hold values from 0 to 65535
Outputs:
- weight_grad: float32 [256, 256], replicated
- prev_grad: bfloat16 [16384, 256], P(('row', 'col'))
Inputs may be any that keep to these rules, and one draw needn't show every extreme that they name: `tile_coords`: within one block, all 512 slots name distinct tile positions; tile rows are below 16 and tile columns below 32. `tile_count`: slots at or beyond a block's count are ignored; some block uses all 512 slots.
All inputs are finite; a program needn't handle non-finite values.
Results may differ from a plain program's by a relative error of at most 0.0049.
Values may be sent and summed in bfloat16 or wider, within the bound.
A program may use at most 128 MiB of HBM per device.

v0:
```python
import math

import jax
import jax.numpy as jnp
from jax import lax
from jax.sharding import PartitionSpec as P

TILE = 128


def unpack(packed):
    shift_list = jnp.arange(16, dtype=jnp.int32)
    bit_values = jnp.right_shift(packed[:, :, None], shift_list[None, None, :]) & 1
    return bit_values.reshape(packed.shape[0], packed.shape[1] * 16)


def total_weight(weight_part, norm_scale):
    return lax.psum(weight_part, ("row", "col")) * norm_scale


def shards(out_grad, out_bits, agg_saved, weight, tiles, tile_coords, tile_count, in_bits):
    row_total = lax.axis_size("row")
    col_total = lax.axis_size("col")
    rows_dev, features = out_grad.shape
    node_total = rows_dev * row_total * col_total
    masked_grad = jnp.where(unpack(out_bits) == 1, out_grad, jnp.zeros_like(out_grad))
    weight_part = lax.dot_general(
        agg_saved, masked_grad, (((0,), (0,)), ((), ())), preferred_element_type=jnp.float32
    )
    hidden_grad = lax.dot_general(
        masked_grad, weight, (((1,), (1,)), ((), ())), preferred_element_type=jnp.float32
    ).astype(jnp.bfloat16)
    gathered = lax.all_gather(hidden_grad, "col", axis=0, tiled=True)
    row_count = gathered.shape[0] // TILE
    row_flat = gathered.reshape(row_count, TILE * features)
    own_tiles = tiles[0, 0]
    own_coords = tile_coords[0, 0]
    tile_total = tile_count[0, 0]
    slot_total = own_tiles.shape[0]
    group_size = min(64, slot_total)
    col_tiles = row_total * rows_dev // TILE
    group_starts = jnp.arange(slot_total // group_size, dtype=jnp.int32) * group_size
    row_ids = jnp.arange(row_count, dtype=jnp.int32)
    norm_scale = 1.0 / math.sqrt(node_total)
    window_ids = jnp.arange(col_tiles, dtype=jnp.int32)

    def scan_group(partial_value, first_slot):
        tile_block = lax.dynamic_slice_in_dim(own_tiles, first_slot, group_size, 0)
        block_coords = lax.dynamic_slice_in_dim(own_coords, first_slot, group_size, 0)
        select = (block_coords[:, 0][:, None] == row_ids[None, :]).astype(jnp.bfloat16)
        picked = jnp.dot(select, row_flat, preferred_element_type=jnp.float32).astype(jnp.bfloat16)
        picked = picked.reshape(group_size, TILE, features)
        products = jnp.einsum(
            "kij,kih->kjh", tile_block, picked, preferred_element_type=jnp.float32
        )
        target = block_coords[:, 1] - 0
        alive_mask = first_slot + jnp.arange(group_size, dtype=jnp.int32) < tile_total
        placing = (window_ids[:, None] == target[None, :]) & alive_mask[None, :]
        placing = placing.astype(jnp.float32)
        added = jnp.dot(
            placing,
            products.reshape(group_size, TILE * features),
            precision=lax.Precision.HIGHEST,
            preferred_element_type=jnp.float32,
        )
        return (partial_value + added, None)

    zero_sums = jnp.zeros((col_tiles, TILE * features), jnp.float32)
    partial_value, unused = lax.scan(scan_group, zero_sums, group_starts)
    flat_sums = partial_value.reshape(col_tiles * TILE, features)
    summed = lax.psum_scatter(flat_sums, "row", scatter_dimension=0, tiled=True)
    weight_grad = total_weight(weight_part, norm_scale)
    prev_grad = jnp.where(unpack(in_bits) == 1, summed, jnp.zeros_like(summed)).astype(jnp.bfloat16)
    return (weight_grad, prev_grad)


def solution(mesh):
    return jax.shard_map(
        shards,
        mesh=mesh,
        in_specs=(
            P(("row", "col"), None),
            P(("row", "col"), None),
            P(("row", "col"), None),
            P(),
            P("row", "col", None, None, None),
            P("row", "col", None, None),
            P("row", "col"),
            P(("row", "col"), None),
        ),
        out_specs=(P(), P(("row", "col"), None)),
        check_vma=False,
    )
```

profile of v0, /device:TPU:0, one launch (start us, length us, event | category | flops | bytes accessed | tf_op | source)
XLA Modules:
  0.0 335.4 jit_solution(15762968083040083463)
XLA Ops:
  10.2 1.9 convolution_convert_fusion.1
  13.2 22.4 %copy.19 = bf16[1,1,512,128,128]{3,4,2,1,0:T(8,128)(2,1)} copy(bf16[1,1,512,128,128]{4,3,2,1,0:T(8,128)(2,1)} %param.14) | data formatting | bytes 33554432 | tf_op args[4]
  35.6 6.0 %all-gather.2.cloned.1.call-done = bf16[2048,256]{1,0:T(8,128)(2,1)} async-done(((bf16[512,256]{1,0:T(8,128)(2,1)}), bf16[2048,256]{1,0:T(8,128)(2,1)}) %all-gather.2.cloned.1.call-update) | async-done | bytes 1048592 | tf_op jit(solution)/shard_map/all_gather | solution.py:33
  41.7 1.6 reshape.32
  43.2 221.7 %while.11 = (s32[]{:T(128)}, f32[32,32768]{1,0:T(8,128)}, s32[8]{0:T(128)S(1)}, s32[512,2]{0,1:T(2,128)}, s32[]{:T(128)}, /*index=5*/bf16[512,128,128]{1,2,0:T(8...) while((s32[]{:T(128)}, f32[32,32768]{1,0:T(8,128)}, s32[8]{0:T(128)S(1)}, ...), condition=%wide.region_2.3_spmd.clone, body=%wide.region_1.2_spmd.clone.sunk | while | flops 1413485696 | bytes 61868840 | solution.py:69
  46.5 1.3 convolution_convert_fusion.3
  48.9 2.9 fusion.35
  51.8 8.0 %copy.28 = f32[8,8,128,256]{3,1,2,0:T(8,128)} copy(f32[8,8,128,256]{3,2,1,0:T(8,128)S(1)} %bitcast.56) | data formatting | bytes 16777216 | tf_op jit(solution)/shard_map/while
  59.7 1.3 add_compare_fusion.2
  61.1 8.9 %convolution_add_fusion.2 = f32[32,32768]{1,0:T(8,128)} fusion(f32[64,32768]{1,0:T(8,128)} %bitcast.55, f32[32,32768]{1,0:T(8,128)} %get-tuple-element.158, pred[]{:T(512)S(6)} %compare.3, s32[64]{0:T(128)S(1)} %get-tuple-element.146, pred[64]{0:T(512)(128)(4,1)S(1)} %add_compare_fusion.2), kind=kOutput, calls=%fused_computation.3.clone.1 | convolution fusion | flops 807407616 | bytes 16777536 | tf_op jit(solution)/shard_map/while/body/eval_jaxpr/dot_general | solution.py:60
  73.3 1.3 convolution_convert_fusion.3
  75.6 2.9 fusion.35
  78.5 8.0 %copy.28 = f32[8,8,128,256]{3,1,2,0:T(8,128)} copy(f32[8,8,128,256]{3,2,1,0:T(8,128)S(1)} %bitcast.56) | data formatting | bytes 16777216 | tf_op jit(solution)/shard_map/while
  86.5 1.3 add_compare_fusion.2
  87.8 10.1 %convolution_add_fusion.2 = f32[32,32768]{1,0:T(8,128)} fusion(f32[64,32768]{1,0:T(8,128)} %bitcast.55, f32[32,32768]{1,0:T(8,128)} %get-tuple-element.158, pred[]{:T(512)S(6)} %compare.3, s32[64]{0:T(128)S(1)} %get-tuple-element.146, pred[64]{0:T(512)(128)(4,1)S(1)} %add_compare_fusion.2), kind=kOutput, calls=%fused_computation.3.clone.1 | convolution fusion | flops 807407616 | bytes 16777536 | tf_op jit(solution)/shard_map/while/body/eval_jaxpr/dot_general | solution.py:60
  101.2 1.3 convolution_convert_fusion.3
  103.6 2.9 fusion.35
  106.5 8.0 %copy.28 = f32[8,8,128,256]{3,1,2,0:T(8,128)} copy(f32[8,8,128,256]{3,2,1,0:T(8,128)S(1)} %bitcast.56) | data formatting | bytes 16777216 | tf_op jit(solution)/shard_map/while
  114.4 1.3 add_compare_fusion.2
  115.7 9.9 %convolution_add_fusion.2 = f32[32,32768]{1,0:T(8,128)} fusion(f32[64,32768]{1,0:T(8,128)} %bitcast.55, f32[32,32768]{1,0:T(8,128)} %get-tuple-element.158, pred[]{:T(512)S(6)} %compare.3, s32[64]{0:T(128)S(1)} %get-tuple-element.146, pred[64]{0:T(512)(128)(4,1)S(1)} %add_compare_fusion.2), kind=kOutput, calls=%fused_computation.3.clone.1 | convolution fusion | flops 807407616 | bytes 16777536 | tf_op jit(solution)/shard_map/while/body/eval_jaxpr/dot_general | solution.py:60
  128.9 1.3 convolution_convert_fusion.3
  131.3 2.9 fusion.35
  134.2 8.0 %copy.28 = f32[8,8,128,256]{3,1,2,0:T(8,128)} copy(f32[8,8,128,256]{3,2,1,0:T(8,128)S(1)} %bitcast.56) | data formatting | bytes 16777216 | tf_op jit(solution)/shard_map/while
  142.1 1.3 add_compare_fusion.2
  143.4 10.1 %convolution_add_fusion.2 = f32[32,32768]{1,0:T(8,128)} fusion(f32[64,32768]{1,0:T(8,128)} %bitcast.55, f32[32,32768]{1,0:T(8,128)} %get-tuple-element.158, pred[]{:T(512)S(6)} %compare.3, s32[64]{0:T(128)S(1)} %get-tuple-element.146, pred[64]{0:T(512)(128)(4,1)S(1)} %add_compare_fusion.2), kind=kOutput, calls=%fused_computation.3.clone.1 | convolution fusion | flops 807407616 | bytes 16777536 | tf_op jit(solution)/shard_map/while/body/eval_jaxpr/dot_general | solution.py:60
  156.8 1.3 convolution_convert_fusion.3
  159.2 2.9 fusion.35
  162.1 8.0 %copy.28 = f32[8,8,128,256]{3,1,2,0:T(8,128)} copy(f32[8,8,128,256]{3,2,1,0:T(8,128)S(1)} %bitcast.56) | data formatting | bytes 16777216 | tf_op jit(solution)/shard_map/while
  170.0 1.3 add_compare_fusion.2
  171.3 10.1 %convolution_add_fusion.2 = f32[32,32768]{1,0:T(8,128)} fusion(f32[64,32768]{1,0:T(8,128)} %bitcast.55, f32[32,32768]{1,0:T(8,128)} %get-tuple-element.158, pred[]{:T(512)S(6)} %compare.3, s32[64]{0:T(128)S(1)} %get-tuple-element.146, pred[64]{0:T(512)(128)(4,1)S(1)} %add_compare_fusion.2), kind=kOutput, calls=%fused_computation.3.clone.1 | convolution fusion | flops 807407616 | bytes 16777536 | tf_op jit(solution)/shard_map/while/body/eval_jaxpr/dot_general | solution.py:60
  184.7 1.3 convolution_convert_fusion.3
  187.1 2.9 fusion.35
  190.0 8.0 %copy.28 = f32[8,8,128,256]{3,1,2,0:T(8,128)} copy(f32[8,8,128,256]{3,2,1,0:T(8,128)S(1)} %bitcast.56) | data formatting | bytes 16777216 | tf_op jit(solution)/shard_map/while
  197.9 1.3 add_compare_fusion.2
  199.2 9.9 %convolution_add_fusion.2 = f32[32,32768]{1,0:T(8,128)} fusion(f32[64,32768]{1,0:T(8,128)} %bitcast.55, f32[32,32768]{1,0:T(8,128)} %get-tuple-element.158, pred[]{:T(512)S(6)} %compare.3, s32[64]{0:T(128)S(1)} %get-tuple-element.146, pred[64]{0:T(512)(128)(4,1)S(1)} %add_compare_fusion.2), kind=kOutput, calls=%fused_computation.3.clone.1 | convolution fusion | flops 807407616 | bytes 16777536 | tf_op jit(solution)/shard_map/while/body/eval_jaxpr/dot_general | solution.py:60
  212.4 1.3 convolution_convert_fusion.3
  214.8 2.9 fusion.35
  217.6 8.0 %copy.28 = f32[8,8,128,256]{3,1,2,0:T(8,128)} copy(f32[8,8,128,256]{3,2,1,0:T(8,128)S(1)} %bitcast.56) | data formatting | bytes 16777216 | tf_op jit(solution)/shard_map/while
  225.6 1.3 add_compare_fusion.2
  226.9 10.1 %convolution_add_fusion.2 = f32[32,32768]{1,0:T(8,128)} fusion(f32[64,32768]{1,0:T(8,128)} %bitcast.55, f32[32,32768]{1,0:T(8,128)} %get-tuple-element.158, pred[]{:T(512)S(6)} %compare.3, s32[64]{0:T(128)S(1)} %get-tuple-element.146, pred[64]{0:T(512)(128)(4,1)S(1)} %add_compare_fusion.2), kind=kOutput, calls=%fused_computation.3.clone.1 | convolution fusion | flops 807407616 | bytes 16777536 | tf_op jit(solution)/shard_map/while/body/eval_jaxpr/dot_general | solution.py:60
  240.3 1.3 convolution_convert_fusion.3
  242.7 2.9 fusion.35
  245.5 8.0 %copy.28 = f32[8,8,128,256]{3,1,2,0:T(8,128)} copy(f32[8,8,128,256]{3,2,1,0:T(8,128)S(1)} %bitcast.56) | data formatting | bytes 16777216 | tf_op jit(solution)/shard_map/while
  253.5 1.3 add_compare_fusion.2
  254.8 10.1 %convolution_add_fusion.2 = f32[32,32768]{1,0:T(8,128)} fusion(f32[64,32768]{1,0:T(8,128)} %bitcast.55, f32[32,32768]{1,0:T(8,128)} %get-tuple-element.158, pred[]{:T(512)S(6)} %compare.3, s32[64]{0:T(128)S(1)} %get-tuple-element.146, pred[64]{0:T(512)(128)(4,1)S(1)} %add_compare_fusion.2), kind=kOutput, calls=%fused_computation.3.clone.1 | convolution fusion | flops 807407616 | bytes 16777536 | tf_op jit(solution)/shard_map/while/body/eval_jaxpr/dot_general | solution.py:60
  264.9 4.9 %reshape.33 = f32[4096,256]{1,0:T(8,128)} reshape(f32[32,32768]{1,0:T(8,128)} %get-tuple-element.49) | data formatting | bytes 8388608 | tf_op jit(solution)/shard_map/reshape | solution.py:70
  269.8 5.7 %copy.20 = f32[4096,256]{0,1:T(8,128)} copy(f32[4096,256]{1,0:T(8,128)} %reshape.33) | data formatting | bytes 8388608 | tf_op jit(solution)/shard_map/reshape | solution.py:70
  277.4 48.5 %reduce-scatter.2.cloned.1.call-done = f32[512,256]{0,1:T(8,128)} async-done(((f32[4096,256]{0,1:T(8,128)}), f32[512,256]{0,1:T(8,128)}) %reduce-scatter.2.cloned.1.call-update) | async-done | bytes 524304 | tf_op jit(solution)/shard_map/reduce_scatter | solution.py:71
  (56 shorter events, 26.7 us)
Async XLA Ops:
  8.0 4.1 %copy-start = (bf16[512,256]{1,0:T(8,128)(2,1)S(1)}, bf16[512,256]{1,0:T(8,128)(2,1)}, u32[]{:S(2)}) copy-start(bf16[512,256]{1,0:T(8,128)(2,1)} %param.12) | copy-start | bytes 786436
  8.0 33.6 %all-gather.2.cloned.1.call-start = ((), (), s32[]{:S(2)}) async-start(), calls=%async_computation.2 | async-start | bytes 1310720 | tf_op jit(solution)/shard_map/all_gather | solution.py:33
  12.1 263.5 %all-reduce.2.cloned.1.call-start = ((), (), s32[]{:S(2)}) async-start(), calls=%async_computation.1 | async-start | bytes 524288 | tf_op jit(solution)/shard_map/psum | solution.py:18
  13.1 312.8 %reduce-scatter.2.cloned.1.call-start = ((), (), s32[]{:S(2)}) async-start(), calls=%async_computation.3 | async-start | bytes 4718592 | tf_op jit(solution)/shard_map/reduce_scatter | solution.py:71
  269.8 58.1 %copy-start.1 = (bf16[512,256]{1,0:T(8,128)(2,1)S(1)}, bf16[512,256]{1,0:T(8,128)(2,1)}, u32[]{:S(2)}) copy-start(bf16[512,256]{1,0:T(8,128)(2,1)} %param.12) | copy-start | bytes 786436
  275.5 50.4 %copy-start.2 = (s32[512,16]{0,1:T(8,128)S(1)}, s32[512,16]{0,1:T(8,128)}, u32[]{:S(2)}) copy-start(s32[512,16]{0,1:T(8,128)} %param.17) | copy-start | bytes 98308
Sparse Core Ops, SparseCore 0:
  12.2 29.4 all-gather.1
  275.6 50.1 reduce-scatter.1
Sparse Core Ops, SparseCore 1:
  18.6 128.3 all-reduce.1
where the time goes:
time: 337 us; the launch traced here: 335 us
  local copies, waits for them, and re-layouts  121 us (36%)
  matrix products  115 us (34%)
  waiting for transfers between devices  54.6 us (16%)
  loops' own time  15.8 us (5%)
  between operations  15.6 us (5%)
  other arithmetic  13.5 us (4%)
    dot_general x8, matrix products, scan_group(): jnp.dot(placing, products.reshape(group_size, TILE * features), precision...  79.1 us
    while x16, local copies, waits for them, and re-layouts  72.5 us
    reduce_scatter x1, waiting for transfers between devices, shards(): summed = lax.psum_scatter(flat_sums, 'row', scatter_dimension=0, tiled=True)  48.5 us
    unnamed x10, local copies, waits for them, and re-layouts  25.2 us
    dot_general x8, matrix products, scan_group(): jnp.einsum('kij,kih->kjh', tile_block, picked, preferred_element_type=jnp...  22.8 us
    another operation x1, loops' own time, shards(): partial_value, unused = lax.scan(scan_group, zero_sums, group_starts)  15.8 us
    reshape x2, local copies, waits for them, and re-layouts, shards(): flat_sums = partial_value.reshape(col_tiles * TILE, features)  10.6 us
    lt x8, other arithmetic, scan_group(): first_slot + jnp.arange(group_size, dtype=jnp.int32) < tile_total  10.4 us
  transfers between devices with their start and end apart: 3, of which 2 were waited for; matrix products, arithmetic and copies ran while one was open for 73% of the time, Pallas kernels for 0%

commit v1 on v0

v1 whole, which is shorter than its diff:
```python
import functools
import math

import jax
import jax.numpy as jnp
from jax import lax
from jax.experimental import pallas as pl
from jax.experimental.pallas import tpu as pltpu
from jax.sharding import PartitionSpec as P

TILE = 128
PAIR = 2 * TILE
PARTS = 2
MESH = pl.DeviceIdType.MESH
F32 = jnp.float32
BF16 = jnp.bfloat16


def bit_mask(bits, features):
    words = bits.shape[1]
    low = (bits & 255).astype(F32).astype(BF16)
    high = ((bits >> 8) & 255).astype(F32).astype(BF16)
    feature = lax.broadcasted_iota(jnp.int32, (words, features), 1)
    word = lax.broadcasted_iota(jnp.int32, (words, features), 0)
    own = (feature >> 4) == word
    in_low = (feature & 15) < 8
    pick_low = jnp.where(own & in_low, 1.0, 0.0).astype(BF16)
    pick_high = jnp.where(own & ~in_low, 1.0, 0.0).astype(BF16)
    byte = jnp.dot(low, pick_low, preferred_element_type=F32)
    byte += jnp.dot(high, pick_high, preferred_element_type=F32)
    shift = lax.broadcasted_iota(jnp.int32, (bits.shape[0], features), 1) & 7
    return (byte.astype(jnp.int32) >> shift) & 1


def prepare(scale, grad_ref, bits_ref, agg_ref, weight_ref, part_ref, hidden_ref):
    mask = bit_mask(bits_ref[...], grad_ref.shape[1])
    masked = jnp.where(mask == 1, grad_ref[...].astype(F32), 0.0).astype(BF16)
    hidden_ref[...] = lax.dot_general(
        weight_ref[...], masked, (((1,), (1,)), ((), ())), preferred_element_type=F32
    ).astype(BF16)
    part_ref[...] = scale * lax.dot_general(
        agg_ref[...], masked, (((0,), (0,)), ((), ())), preferred_element_type=F32
    )


def flip_bits(index, bits, total):
    result = index
    step = 1
    while step < total:
        if bits & step:
            result = result + step * (1 - 2 * ((index // step) % 2))
        step *= 2
    return result


def exchange(
    rows, cols, hidden_ref, part_ref, tiles_ref, table_ref, bits_ref, out_ref, weight_ref,
    tile_buf, gathered, acc, pair_out, pair_in, chain_out, chain_in, mask_buf,
    by_col, col_sum, by_row, row_sum, col_total, total_buf,
    w1_send, w1_recv, w2_send, w2_recv, w3_send, w3_recv, w4_send, w4_recv,
    tile_sem, hid_send, hid_recv, pair_send, pair_recv, chain_send, chain_recv,
):
    slots = tiles_ref.shape[0]
    features, nodes = hidden_ref.shape
    row_tiles = nodes // TILE
    col_tiles = rows * nodes // TILE
    pairs_per = nodes // PAIR
    part = features // PARTS
    chips = rows // 2
    my_row = lax.axis_index("row")
    my_col = lax.axis_index("col")
    place = my_row // 2
    core = my_row % 2
    partner = place * 2 + 1 - core

    loads = []
    chunk = slots // 8
    for piece in range(8):
        span = pl.ds(piece * chunk, chunk)
        load = pltpu.make_async_copy(tiles_ref.at[span], tile_buf.at[span], tile_sem.at[piece])
        load.start()
        loads.append(load)

    barrier = pltpu.get_barrier_semaphore()
    peers = [flip_bits(my_col, k, cols) for k in range(cols)]
    for k in range(1, cols):
        pl.semaphore_signal(barrier, inc=1, device_id=(my_row, peers[k]), device_id_type=MESH)
    mates = [(my_row + i) % rows for i in range(rows)]
    for i in range(1, rows):
        pl.semaphore_signal(barrier, inc=1, device_id=(mates[i], my_col), device_id_type=MESH)
    pl.semaphore_wait(barrier, rows + cols - 2)

    sends = []
    for k in range(1, cols):
        copy = pltpu.make_async_remote_copy(
            src_ref=hidden_ref, dst_ref=gathered.at[my_col],
            send_sem=hid_send.at[k], recv_sem=hid_recv.at[my_col],
            device_id=(my_row, peers[k]), device_id_type=MESH,
        )
        copy.start()
        sends.append(copy)

    gathered[my_col] = hidden_ref[...]
    tile_buf[slots] = jnp.zeros((TILE, TILE), BF16)
    mask_buf[...] = bit_mask(bits_ref[...], features).astype(F32)
    for load in loads:
        load.wait()

    def product(source, pair):
        strips = []
        for i in range(row_tiles):
            base = (source * row_tiles + i) * col_tiles + 2 * pair
            strips.append(jnp.concatenate([tile_buf[table_ref[base]], tile_buf[table_ref[base + 1]]], axis=1))
        return jnp.dot(gathered[source], jnp.concatenate(strips, axis=0), preferred_element_type=F32)

    def hid_wait(k):
        pltpu.make_async_remote_copy(
            src_ref=hidden_ref, dst_ref=gathered.at[peers[k]],
            send_sem=hid_send.at[k], recv_sem=hid_recv.at[peers[k]],
            device_id=(my_row, peers[k]), device_id_type=MESH,
        ).wait_recv()

    for k in range(cols - 1):
        if k:
            hid_wait(k)

        @pl.loop(0, col_tiles // 2)
        def _(pair, k=k):
            value = product(peers[k], pair)
            if k:
                value += acc[pair]
            acc[pair] = value

    hid_wait(cols - 1)

    band = features // cols
    owners = min(rows, band // 8)
    strip = band // owners

    def w1_copy(k):
        return pltpu.make_async_remote_copy(
            src_ref=part_ref.at[pl.ds(pl.multiple_of(peers[k] * band, 8), band)], dst_ref=by_col.at[my_col],
            send_sem=w1_send.at[k], recv_sem=w1_recv.at[my_col],
            device_id=(my_row, peers[k]), device_id_type=MESH,
        )

    def w2_copy(i):
        return pltpu.make_async_remote_copy(
            src_ref=col_sum.at[pl.ds(pl.multiple_of(mates[i] * strip, 8), strip)], dst_ref=by_row.at[my_row],
            send_sem=w2_send.at[i], recv_sem=w2_recv.at[my_row],
            device_id=(mates[i], my_col), device_id_type=MESH,
        )

    def w3_copy(i):
        return pltpu.make_async_remote_copy(
            src_ref=row_sum, dst_ref=col_total.at[pl.ds(pl.multiple_of(my_row * strip, 8), strip)],
            send_sem=w3_send.at[i], recv_sem=w3_recv.at[my_row],
            device_id=(mates[i], my_col), device_id_type=MESH,
        )

    def w4_copy(k):
        return pltpu.make_async_remote_copy(
            src_ref=col_total, dst_ref=total_buf.at[pl.ds(pl.multiple_of(my_col * band, 8), band)],
            send_sem=w4_send.at[k], recv_sem=w4_recv.at[my_col],
            device_id=(my_row, peers[k]), device_id_type=MESH,
        )

    def landed(ref, sem):
        pltpu.make_async_copy(ref, ref, sem).wait()

    def weight_one():
        for k in range(1, cols):
            w1_copy(k).start()

    def weight_two():
        total = part_ref[pl.ds(pl.multiple_of(my_col * band, 8), band), :]
        for k in range(1, cols):
            landed(by_col.at[peers[k]], w1_recv.at[peers[k]])
            total += by_col[peers[k]]
        col_sum[...] = total
        for i in range(1, rows):
            @pl.when(mates[i] < owners)
            def _():
                w2_copy(i).start()

    def weight_three():
        @pl.when(my_row < owners)
        def _():
            mine = pl.ds(pl.multiple_of(my_row * strip, 8), strip)
            total = col_sum[mine, :]
            for i in range(1, rows):
                landed(by_row.at[mates[i]], w2_recv.at[mates[i]])
                total += by_row[mates[i]]
            row_sum[...] = total
            col_total[mine, :] = total
            for i in range(1, rows):
                w3_copy(i).start()

    def weight_four():
        for i in range(1, rows):
            @pl.when(mates[i] < owners)
            def _():
                landed(col_total.at[pl.ds(pl.multiple_of(mates[i] * strip, 8), strip)], w3_recv.at[mates[i]])
        total_buf[pl.ds(pl.multiple_of(my_col * band, 8), band), :] = col_total[...]
        for k in range(1, cols):
            w4_copy(k).start()

    def weight_end():
        for k in range(1, cols):
            landed(total_buf.at[pl.ds(pl.multiple_of(peers[k] * band, 8), band)], w4_recv.at[peers[k]])
        weight_ref[...] = total_buf[...]
        for k in range(1, cols):
            w1_copy(k).wait_send()
            w4_copy(k).wait_send()
        for i in range(1, rows):
            @pl.when(mates[i] < owners)
            def _():
                w2_copy(i).wait_send()

            @pl.when(my_row < owners)
            def _():
                w3_copy(i).wait_send()

    weight_one()

    order = []
    for d in range((chips + 1) // 2):
        order += [chips - 1 - d] + ([d] if d != chips - 1 - d else [])

    def finish(owner):
        for j in range(pairs_per):
            pair = owner * pairs_per + j
            yield j, acc[pair] + product(peers[cols - 1], pair)

    def pair_copy(spot):
        return pltpu.make_async_remote_copy(
            src_ref=pair_out.at[spot], dst_ref=pair_in.at[spot],
            send_sem=pair_send.at[spot], recv_sem=pair_recv.at[spot],
            device_id=(partner, my_col), device_id_type=MESH,
        )

    for spot in order:
        for j, value in finish(2 * spot + 1 - core):
            pair_out[spot, :, pl.ds(j * PAIR, PAIR)] = value.astype(BF16)
        pair_copy(spot).start()
    for spot in order:
        for j, value in finish(2 * spot + core):
            acc[(2 * spot + core) * pairs_per + j] = value

    def chain_copy(way, spot, p):
        return pltpu.make_async_remote_copy(
            src_ref=chain_out.at[way, spot, p], dst_ref=chain_in.at[way, spot, p],
            send_sem=chain_send.at[way, spot, p], recv_sem=chain_recv.at[way, spot, p],
            device_id=(my_row + 2 - 4 * way, my_col), device_id_type=MESH,
        )

    def local_sum(spot, p):
        first = (2 * spot + core) * pairs_per
        own = jnp.concatenate(
            [acc[first + j, p * part:(p + 1) * part, :] for j in range(pairs_per)], axis=1
        )
        return own + pair_in[spot, p * part:(p + 1) * part, :].astype(F32)

    def hop(way, d):
        spot = (1 - way) * (chips - 1 - d) + way * d
        ahead = (1 - 2 * way) * (spot - place)
        behind = (1 - way) * place + way * (chips - 1 - place)

        @pl.when(ahead > 0)
        def _():
            for p in range(PARTS):
                @pl.when(behind > 0)
                def _():
                    chain_copy(way, spot, p).wait_recv()
                    total = local_sum(spot, p) + chain_in[way, spot, p].astype(F32)
                    chain_out[way, spot, p] = total.astype(BF16)

                @pl.when(behind == 0)
                def _():
                    chain_out[way, spot, p] = local_sum(spot, p).astype(BF16)

                chain_copy(way, spot, p).start()

    way = place // ((chips + 1) // 2)
    for spot in order:
        pair_copy(spot).wait_recv()
    weight_two()
    for d in range(chips - 1):
        hop(way, d)
        if d == 0:
            weight_three()
        hop(1 - way, d)
        if d == 0:
            weight_four()

    for p in range(PARTS):
        rows_p = pl.ds(p * part, part)
        first = (2 * place + core) * pairs_per
        for j in range(pairs_per):
            acc[first + j, rows_p, :] += pair_in[place, rows_p, pl.ds(j * PAIR, PAIR)].astype(F32)

        @pl.when(place > 0)
        def _():
            chain_copy(0, place, p).wait_recv()
            for j in range(pairs_per):
                acc[first + j, rows_p, :] += chain_in[0, place, p, :, pl.ds(j * PAIR, PAIR)].astype(F32)

        @pl.when(place < chips - 1)
        def _():
            chain_copy(1, place, p).wait_recv()
            for j in range(pairs_per):
                acc[first + j, rows_p, :] += chain_in[1, place, p, :, pl.ds(j * PAIR, PAIR)].astype(F32)

        for j in range(pairs_per):
            area = (pl.ds(j * PAIR, PAIR), rows_p)
            out_ref[area] = jnp.where(mask_buf[area] > 0.5, acc[first + j, rows_p, :].T, 0.0).astype(BF16)

    weight_end()
    for copy in sends:
        copy.wait_send()
    for spot in order:
        pair_copy(spot).wait_send()
    for spot in range(chips):
        for p in range(PARTS):
            @pl.when(spot > place)
            def _():
                chain_copy(0, spot, p).wait_send()

            @pl.when(spot < place)
            def _():
                chain_copy(1, spot, p).wait_send()


def shards(out_grad, out_bits, agg_saved, weight, tiles, tile_coords, tile_count, in_bits):
    rows = lax.axis_size("row")
    cols = lax.axis_size("col")
    nodes, features = out_grad.shape
    scale = 1.0 / math.sqrt(nodes * rows * cols)
    slots = tiles.shape[2]
    row_tiles = cols * nodes // TILE
    col_tiles = rows * nodes // TILE
    chips = rows // 2
    part = features // PARTS
    vmem = pl.BlockSpec(memory_space=pltpu.VMEM)

    weight_part, hidden = pl.pallas_call(
        functools.partial(prepare, scale),
        out_shape=(
            jax.ShapeDtypeStruct((features, features), F32),
            jax.ShapeDtypeStruct((features, nodes), BF16),
        ),
        in_specs=[vmem] * 4,
        out_specs=(vmem, vmem),
        compiler_params=pltpu.CompilerParams(vmem_limit_bytes=32 * 2**20),
        name="prepare",
    )(out_grad, out_bits, agg_saved, weight)

    spot = tile_coords[0, 0, :, 0] * col_tiles + tile_coords[0, 0, :, 1]
    slot = jnp.arange(slots, dtype=jnp.int32)
    spot = jnp.where(slot < tile_count[0, 0], spot, -1)
    hit = spot[:, None] == jnp.arange(row_tiles * col_tiles, dtype=jnp.int32)[None, :]
    table = jnp.min(jnp.where(hit, slot[:, None], slots), axis=0)

    dma = pltpu.SemaphoreType.DMA
    band = features // cols
    strip = band // min(rows, band // 8)
    prev_grad, weight_grad = pl.pallas_call(
        functools.partial(exchange, rows, cols),
        out_shape=(
            jax.ShapeDtypeStruct((nodes, features), BF16),
            jax.ShapeDtypeStruct((features, features), F32),
        ),
        in_specs=[vmem, vmem, pl.BlockSpec(memory_space=pl.ANY), pl.BlockSpec(memory_space=pltpu.SMEM), vmem],
        out_specs=(vmem, vmem),
        scratch_shapes=[
            pltpu.VMEM((slots + 1, TILE, TILE), BF16),
            pltpu.VMEM((cols, features, nodes), BF16),
            pltpu.VMEM((col_tiles // 2, features, PAIR), F32),
            pltpu.VMEM((chips, features, nodes), BF16),
            pltpu.VMEM((chips, features, nodes), BF16),
            pltpu.VMEM((2, chips, PARTS, part, nodes), BF16),
            pltpu.VMEM((2, chips, PARTS, part, nodes), BF16),
            pltpu.VMEM((nodes, features), F32),
            pltpu.VMEM((cols, band, features), F32),
            pltpu.VMEM((band, features), F32),
            pltpu.VMEM((rows, strip, features), F32),
            pltpu.VMEM((strip, features), F32),
            pltpu.VMEM((band, features), F32),
            pltpu.VMEM((features, features), F32),
            dma((cols,)),
            dma((cols,)),
            dma((rows,)),
            dma((rows,)),
            dma((rows,)),
            dma((rows,)),
            dma((cols,)),
            dma((cols,)),
            dma((8,)),
            dma((cols,)),
            dma((cols,)),
            dma((chips,)),
            dma((chips,)),
            dma((2, chips, PARTS)),
            dma((2, chips, PARTS)),
        ],
        compiler_params=pltpu.CompilerParams(
            collective_id=0, has_side_effects=True, vmem_limit_bytes=56 * 2**20
        ),
        cost_estimate=pl.CostEstimate(
            flops=2 * row_tiles * col_tiles * TILE * TILE * features,
            bytes_accessed=slots * TILE * TILE * 2, transcendentals=0,
        ),
        name="exchange",
    )(hidden, weight_part, tiles[0, 0], table, in_bits)
    return weight_grad, prev_grad


def solution(mesh):
    return jax.shard_map(
        shards,
        mesh=mesh,
        in_specs=(
            P(("row", "col"), None),
            P(("row", "col"), None),
            P(("row", "col"), None),
            P(),
            P("row", "col", None, None, None),
            P("row", "col", None, None),
            P("row", "col"),
            P(("row", "col"), None),
        ),
        out_specs=(P(), P(("row", "col"), None)),
        check_vma=False,
    )
```

time: 337 us -> 68.3 us (0.20)
  matrix products: 115 us -> 0 us
  local copies, waits for them, and re-layouts: 121 us -> 10 us
  Pallas kernels: 0 us -> 54.9 us
  waiting for transfers between devices: 54.6 us -> 0 us
  loops' own time: 15.8 us -> 0 us
  between operations: 15.6 us -> 1.32 us
  other arithmetic: 13.5 us -> 1.58 us
    dot_general x26 -> x0, matrix products: 115 us -> none  [the longest x8 79.1 us: scan_group(): jnp.dot(placing, products.reshape(group_size, TILE * features), precision...]
    while x16 -> x0, local copies, waits for them, and re-layouts: 72.5 us -> none
    pallas_call x0 -> x2, Pallas kernels: none -> 54.9 us  [the longest x1 54.2 us: shards(): pl.pallas_call(functools.partial(exchange, rows, cols), out_shape=(jax.Sh...]
    reduce_scatter x1 -> x0, waiting for transfers between devices: 48.5 us -> none  [shards(): summed = lax.psum_scatter(flat_sums, 'row', scatter_dimension=0, tiled=True)]
    another operation x1 -> x0, loops' own time: 15.8 us -> none  [shards(): partial_value, unused = lax.scan(scan_group, zero_sums, group_starts)]
    unnamed x10 -> x14, local copies, waits for them, and re-layouts: 25.2 us -> 10 us
    reshape x3 -> x0, local copies, waits for them, and re-layouts: 12.2 us -> none  [the longest x2 10.6 us: shards(): flat_sums = partial_value.reshape(col_tiles * TILE, features)]
    dynamic_slice x16 -> x0, local copies, waits for them, and re-layouts: 10.7 us -> none  [the longest x8 6.08 us: scan_group(): lax.dynamic_slice_in_dim(own_coords, first_slot, group_size, 0)]
  transfers between devices with their start and end apart: 3 -> 0, of which waited for: 2 -> 0; matrix products, arithmetic and copies ran while one was open for 73% -> 0% of each run, Pallas kernels for 0% -> 0%
where the time goes in v1:
time: 68.3 us; the launch traced here: 67.8 us
  Pallas kernels  54.9 us (80%)
  local copies, waits for them, and re-layouts  10 us (15%)
  other arithmetic  1.58 us (2%)
  between operations  1.32 us (2%)
    pallas_call x1, Pallas kernels, shards(): pl.pallas_call(functools.partial(exchange, rows, cols), out_shape=(jax.Sh...  54.2 us
    unnamed x14, local copies, waits for them, and re-layouts  10 us

profile of v1, /device:TPU:0, one launch (start us, length us, event | category | flops | bytes accessed | tf_op | source)
XLA Modules:
  0.0 67.8 jit_solution(7221340682190487340)
XLA Ops:
  1.3 0.8 %slice_add_fusion = s32[1,1,512,1]{2,3,1,0:T(1,128)S(1)} fusion(s32[1,1,512,2]{2,3,1,0:T(2,128)} %param.13), kind=kLoop, calls=%fused_computation.2 | loop fusion | flops 1024 | bytes 6144 | tf_op jit(solution)/shard_map/add | solution.py:358
  2.1 0.8 %select_reduce_fusion.table_ref = s32[512]{0:T(512)} fusion(s32[512]{0:T(512)S(1)} %fusion), kind=kLoop, calls=%fused_computation | loop fusion | flops 785920 | bytes 4096 | tf_op jit(solution)/shard_map/reduce_min | solution.py:362
  2.9 0.9 %copy.12.bits_ref = s32[512,16]{1,0:T(8,128)S(1)} copy(s32[512,16]{0,1:T(8,128)} %param.9) | data formatting | bytes 65536 | tf_op args[1]
  3.7 1.6 %copy.13.bits_ref = s32[512,16]{1,0:T(8,128)} copy(s32[512,16]{0,1:T(8,128)} %param.15) | data formatting | bytes 65536 | tf_op args[7]
  5.3 0.0 copy-start.2
  5.3 0.9 %copy-done.2 = bf16[512,256]{1,0:T(8,128)(2,1)S(1)} copy-done((bf16[512,256]{1,0:T(8,128)(2,1)S(1)}, bf16[512,256]{1,0:T(8,128)(2,1)}, u32[]{:S(2)}) %copy-start.2) | copy-done | bytes 262168
  6.3 0.0 copy-start.3
  6.3 0.9 %copy-done.3 = bf16[512,256]{1,0:T(8,128)(2,1)S(1)} copy-done((bf16[512,256]{1,0:T(8,128)(2,1)S(1)}, bf16[512,256]{1,0:T(8,128)(2,1)}, u32[]{:S(2)}) %copy-start.3) | copy-done | bytes 262168
  7.2 0.0 copy-start.4
  7.2 0.9 %copy-done.4 = bf16[256,256]{1,0:T(8,128)(2,1)S(1)} copy-done((bf16[256,256]{1,0:T(8,128)(2,1)S(1)}, bf16[256,256]{1,0:T(8,128)(2,1)}, u32[]{:S(2)}) %copy-start.4) | copy-done | bytes 131096
  8.1 0.7 %prepare.1 = (f32[256,256]{1,0:T(8,128)S(1)}, bf16[256,512]{1,0:T(8,128)(2,1)S(1)}) custom-call(bf16[512,256]{1,0:T(8,128)(2,1)S(1)} %copy-done.2, s32[512,16]{1,0:T(8,128)S(1)} %copy.12.bits_ref, bf16[512,256]{1,0:T(8,128)(2,1)S(1)} %copy-done.3, bf16[256,256]{1,0:T(8,128)(2,1)S(1)} %copy-done.4), custom_call_target="tpu_custom_call" | custom-call | tf_op jit(solution)/shard_map/prepare/pallas_call | solution.py:346
  8.8 0.0 copy-start
  8.8 0.7 %copy-done = f32[256,256]{1,0:T(8,128)} copy-done((f32[256,256]{1,0:T(8,128)}, f32[256,256]{1,0:T(8,128)S(1)}, u32[]{:S(2)}) %copy-start) | copy-done | bytes 262168
  9.5 0.0 copy-start.1
  9.5 0.7 %copy-done.1 = bf16[256,512]{1,0:T(8,128)(2,1)} copy-done((bf16[256,512]{1,0:T(8,128)(2,1)}, bf16[256,512]{1,0:T(8,128)(2,1)S(1)}, u32[]{:S(2)}) %copy-start.1) | copy-done | bytes 262168
  10.2 54.2 %exchange.1 = (bf16[512,256]{1,0:T(8,128)(2,1)}, f32[256,256]{1,0:T(8,128)}) custom-call(bf16[256,512]{1,0:T(8,128)(2,1)} %copy-done.1, f32[256,256]{1,0:T(8,128)} %copy-done, bf16[512,128,128]{2,1,0:T(8,128)(2,1)} %bitcast.4, s32[512]{0:T(512)} %select_reduce_fusion.table_ref, s32[512,16]{1,0:T(8,128)} %copy.13.bits_ref), custom_call_target="tpu_custom_call" | custom-call | flops 4294967296 | bytes 16777216 | tf_op jit(solution)/shard_map/exchange/pallas_call | solution.py:367
  64.5 1.7 %copy.17 = f32[256,256]{1,0:T(8,128)} copy(f32[256,256]{1,0:T(8,128)} %get-tuple-element.12) | data formatting | bytes 524288
  66.1 1.7 %copy.18 = bf16[512,256]{1,0:T(8,128)(2,1)} copy(bf16[512,256]{1,0:T(8,128)(2,1)} %get-tuple-element.13) | data formatting | bytes 524288
  (1 shorter events, 0.0 us)
Async XLA Ops:
  5.3 0.9 %copy-start.2 = (bf16[512,256]{1,0:T(8,128)(2,1)S(1)}, bf16[512,256]{1,0:T(8,128)(2,1)}, u32[]{:S(2)}) copy-start(bf16[512,256]{1,0:T(8,128)(2,1)} %grad_ref.1) | copy-start | bytes 786436
  6.3 0.9 %copy-start.3 = (bf16[512,256]{1,0:T(8,128)(2,1)S(1)}, bf16[512,256]{1,0:T(8,128)(2,1)}, u32[]{:S(2)}) copy-start(bf16[512,256]{1,0:T(8,128)(2,1)} %agg_ref.1) | copy-start | bytes 786436
  7.2 0.9 %copy-start.4 = (bf16[256,256]{1,0:T(8,128)(2,1)S(1)}, bf16[256,256]{1,0:T(8,128)(2,1)}, u32[]{:S(2)}) copy-start(bf16[256,256]{1,0:T(8,128)(2,1)} %weight_ref.1) | copy-start | bytes 393220
  8.8 0.7 %copy-start = (f32[256,256]{1,0:T(8,128)}, f32[256,256]{1,0:T(8,128)S(1)}, u32[]{:S(2)}) copy-start(f32[256,256]{1,0:T(8,128)S(1)} %get-tuple-element.7.part_ref) | copy-start | bytes 786436
  9.5 0.7 %copy-start.1 = (bf16[256,512]{1,0:T(8,128)(2,1)}, bf16[256,512]{1,0:T(8,128)(2,1)S(1)}, u32[]{:S(2)}) copy-start(bf16[256,512]{1,0:T(8,128)(2,1)S(1)} %get-tuple-element.6.hidden_ref) | copy-start | bytes 786436

commit v2 on v1

v2 whole, which is shorter than its diff:
```python
import functools
import math

import jax
import jax.numpy as jnp
from jax import lax
from jax.experimental import pallas as pl
from jax.experimental.pallas import tpu as pltpu
from jax.sharding import PartitionSpec as P

TILE = 128
PAIR = 2 * TILE
PARTS = 2
MESH = pl.DeviceIdType.MESH
F32 = jnp.float32
BF16 = jnp.bfloat16


def bit_mask(bits, features, across):
    words, nodes = bits.shape
    low = (bits & 255).astype(F32).astype(BF16)
    high = ((bits >> 8) & 255).astype(F32).astype(BF16)
    feature = lax.broadcasted_iota(jnp.int32, (words, features), 1)
    word = lax.broadcasted_iota(jnp.int32, (words, features), 0)
    own = (feature >> 4) == word
    in_low = (feature & 15) < 8
    pick_low = jnp.where(own & in_low, 1.0, 0.0).astype(BF16)
    pick_high = jnp.where(own & ~in_low, 1.0, 0.0).astype(BF16)

    def place(pick, byte):
        left, right = (pick, byte) if across else (byte, pick)
        return lax.dot_general(left, right, (((0,), (0,)), ((), ())), preferred_element_type=F32)

    byte = place(pick_low, low) + place(pick_high, high)
    shift = lax.broadcasted_iota(jnp.int32, byte.shape, 0 if across else 1) & 7
    return (byte.astype(jnp.int32) >> shift) & 1


def flip_bits(index, bits, total):
    result = index
    step = 1
    while step < total:
        if bits & step:
            result = result + step * (1 - 2 * ((index // step) % 2))
        step *= 2
    return result


def exchange(
    rows, cols, scale, grad_hbm, bits_hbm, agg_hbm, weight_hbm, tiles_ref, coords_hbm, count_ref, inbits_hbm,
    out_ref, weight_ref,
    by_col, col_sum, by_row, row_sum, col_total, total_buf,
    w1_send, w1_recv, w2_send, w2_recv, w3_send, w3_recv, w4_send, w4_recv,
    grad_buf, bits_buf, agg_buf, mat_buf, coords_buf, inbits_buf, table_buf, table_ref, hidden_ref, part_ref, load_sem,
    tile_buf, gathered, acc, pair_out, pair_in, chain_out, chain_in, mask_buf,
    tile_sem, hid_send, hid_recv, pair_send, pair_recv, chain_send, chain_recv,
):
    slots = tiles_ref.shape[0]
    nodes, features = grad_hbm.shape
    row_tiles = nodes // TILE
    col_tiles = rows * nodes // TILE
    positions = cols * row_tiles * col_tiles
    pairs_per = nodes // PAIR
    part = features // PARTS
    chips = rows // 2
    my_row = lax.axis_index("row")
    my_col = lax.axis_index("col")
    place = my_row // 2
    core = my_row % 2
    partner = place * 2 + 1 - core

    barrier = pltpu.get_barrier_semaphore()
    peers = [flip_bits(my_col, k, cols) for k in range(cols)]
    mates = [(my_row + i) % rows for i in range(rows)]
    for k in range(1, cols):
        pl.semaphore_signal(barrier, inc=1, device_id=(my_row, peers[k]), device_id_type=MESH)
    for i in range(1, rows):
        pl.semaphore_signal(barrier, inc=1, device_id=(mates[i], my_col), device_id_type=MESH)

    pairs_in = [
        (bits_hbm, bits_buf), (grad_hbm, grad_buf), (weight_hbm, mat_buf),
        (coords_hbm, coords_buf), (inbits_hbm, inbits_buf), (agg_hbm, agg_buf),
    ]
    inputs = [pltpu.make_async_copy(src, dst, load_sem.at[i]) for i, (src, dst) in enumerate(pairs_in)]
    for load in inputs:
        load.start()
    loads = []
    chunk = slots // 8
    for piece in range(8):
        span = pl.ds(piece * chunk, chunk)
        load = pltpu.make_async_copy(tiles_ref.at[span], tile_buf.at[span], tile_sem.at[piece])
        load.start()
        loads.append(load)

    for load in inputs[:3]:
        load.wait()
    mask = bit_mask(bits_buf[...], features, False)
    masked = jnp.where(mask == 1, grad_buf[...].astype(F32), 0.0).astype(BF16)
    hidden_ref[...] = lax.dot_general(
        mat_buf[...], masked, (((1,), (1,)), ((), ())), preferred_element_type=F32
    ).astype(BF16).reshape(PARTS, part, nodes)
    pl.semaphore_wait(barrier, rows + cols - 2)

    def hid_copy(k, p):
        return pltpu.make_async_remote_copy(
            src_ref=hidden_ref.at[p], dst_ref=gathered.at[my_col, p],
            send_sem=hid_send.at[k, p], recv_sem=hid_recv.at[my_col, p],
            device_id=(my_row, peers[k]), device_id_type=MESH,
        )

    def landed(ref, sem):
        pltpu.make_async_copy(ref, ref, sem).wait()

    for k in range(1, cols):
        hid_copy(k, 0).start()

    gathered[my_col] = hidden_ref[...]
    tile_buf[slots] = jnp.zeros((TILE, TILE), BF16)
    for load in inputs[3:]:
        load.wait()
    spot_of = coords_buf[0:1, :] * col_tiles + coords_buf[1:2, :]
    alive = lax.broadcasted_iota(jnp.int32, (1, slots), 1) < count_ref[0, 0]
    spot_of = jnp.where(alive, spot_of, -1)
    spot_of = jnp.broadcast_to(spot_of, (8, slots)).T[:, 0:1]
    wide = min(512, positions)
    for first in range(0, positions, wide):
        spots = lax.broadcasted_iota(jnp.int32, (slots, wide), 1) + first
        slot = lax.broadcasted_iota(jnp.int32, (slots, wide), 0)
        found = jnp.min(jnp.where(spot_of == spots, slot, slots), axis=0, keepdims=True)
        table_buf[:, first:first + wide] = jnp.minimum(jnp.maximum(found, 0), slots)
    to_scalars = pltpu.make_async_copy(table_buf, table_ref, load_sem.at[len(inputs)])
    to_scalars.start()
    part_ref[...] = scale * lax.dot_general(
        agg_buf[...], masked, (((0,), (0,)), ((), ())), preferred_element_type=F32
    )
    mask_buf[...] = bit_mask(inbits_buf[...], features, True).astype(F32)
    to_scalars.wait()
    for load in loads:
        load.wait()

    def product(source, pair, p):
        strips = []
        for i in range(row_tiles):
            base = (source * row_tiles + i) * col_tiles + 2 * pair
            strips.append(
                jnp.concatenate([tile_buf[table_ref[0, base]], tile_buf[table_ref[0, base + 1]]], axis=1)
            )
        return jnp.dot(gathered[source, p], jnp.concatenate(strips, axis=0), preferred_element_type=F32)

    def add_source(k, p):
        if k:
            landed(gathered.at[peers[k], p], hid_recv.at[peers[k], p])

        @pl.loop(0, col_tiles // 2)
        def _(pair):
            value = product(peers[k], pair, p)
            if k:
                value += acc[p, pair]
            acc[p, pair] = value

    band = features // cols
    owners = min(rows, band // 8)
    strip = band // owners

    def w1_copy(k):
        return pltpu.make_async_remote_copy(
            src_ref=part_ref.at[pl.ds(pl.multiple_of(peers[k] * band, 8), band)], dst_ref=by_col.at[my_col],
            send_sem=w1_send.at[k], recv_sem=w1_recv.at[my_col],
            device_id=(my_row, peers[k]), device_id_type=MESH,
        )

    def w2_copy(i):
        return pltpu.make_async_remote_copy(
            src_ref=col_sum.at[pl.ds(pl.multiple_of(mates[i] * strip, 8), strip)], dst_ref=by_row.at[my_row],
            send_sem=w2_send.at[i], recv_sem=w2_recv.at[my_row],
            device_id=(mates[i], my_col), device_id_type=MESH,
        )

    def w3_copy(i):
        return pltpu.make_async_remote_copy(
            src_ref=row_sum, dst_ref=col_total.at[pl.ds(pl.multiple_of(my_row * strip, 8), strip)],
            send_sem=w3_send.at[i], recv_sem=w3_recv.at[my_row],
            device_id=(mates[i], my_col), device_id_type=MESH,
        )

    def w4_copy(k):
        return pltpu.make_async_remote_copy(
            src_ref=col_total, dst_ref=total_buf.at[pl.ds(pl.multiple_of(my_col * band, 8), band)],
            send_sem=w4_send.at[k], recv_sem=w4_recv.at[my_col],
            device_id=(my_row, peers[k]), device_id_type=MESH,
        )

    def weight_one():
        for k in range(1, cols):
            w1_copy(k).start()

    def weight_two():
        total = part_ref[pl.ds(pl.multiple_of(my_col * band, 8), band), :]
        for k in range(1, cols):
            landed(by_col.at[peers[k]], w1_recv.at[peers[k]])
            total += by_col[peers[k]]
        col_sum[...] = total
        for i in range(1, rows):
            @pl.when(mates[i] < owners)
            def _():
                w2_copy(i).start()

    def weight_three():
        @pl.when(my_row < owners)
        def _():
            mine = pl.ds(pl.multiple_of(my_row * strip, 8), strip)
            total = col_sum[mine, :]
            for i in range(1, rows):
                landed(by_row.at[mates[i]], w2_recv.at[mates[i]])
                total += by_row[mates[i]]
            row_sum[...] = total
            col_total[mine, :] = total
            for i in range(1, rows):
                w3_copy(i).start()

    def weight_four():
        for i in range(1, rows):
            @pl.when(mates[i] < owners)
            def _():
                landed(col_total.at[pl.ds(pl.multiple_of(mates[i] * strip, 8), strip)], w3_recv.at[mates[i]])
        total_buf[pl.ds(pl.multiple_of(my_col * band, 8), band), :] = col_total[...]
        for k in range(1, cols):
            w4_copy(k).start()

    def weight_end():
        for k in range(1, cols):
            landed(total_buf.at[pl.ds(pl.multiple_of(peers[k] * band, 8), band)], w4_recv.at[peers[k]])
        weight_ref[...] = total_buf[...]
        for k in range(1, cols):
            w1_copy(k).wait_send()
            w4_copy(k).wait_send()
        for i in range(1, rows):
            @pl.when(mates[i] < owners)
            def _():
                w2_copy(i).wait_send()

            @pl.when(my_row < owners)
            def _():
                w3_copy(i).wait_send()

    order = []
    for d in range((chips + 1) // 2):
        order += [chips - 1 - d] + ([d] if d != chips - 1 - d else [])
    way = place // ((chips + 1) // 2)

    def pair_copy(spot, p):
        return pltpu.make_async_remote_copy(
            src_ref=pair_out.at[p, spot], dst_ref=pair_in.at[p, spot],
            send_sem=pair_send.at[p, spot], recv_sem=pair_recv.at[p, spot],
            device_id=(partner, my_col), device_id_type=MESH,
        )

    def finish(p):
        landed(gathered.at[peers[cols - 1], p], hid_recv.at[peers[cols - 1], p])
        for spot in order:
            for j in range(pairs_per):
                pair = (2 * spot + 1 - core) * pairs_per + j
                value = acc[p, pair] + product(peers[cols - 1], pair, p)
                pair_out[p, spot, :, pl.ds(j * PAIR, PAIR)] = value.astype(BF16)
            pair_copy(spot, p).start()
        for spot in order:
            for j in range(pairs_per):
                pair = (2 * spot + core) * pairs_per + j
                acc[p, pair] += product(peers[cols - 1], pair, p)

    def pair_wait(p):
        for spot in order:
            pair_copy(spot, p).wait_recv()

    def chain_copy(way, spot, p):
        return pltpu.make_async_remote_copy(
            src_ref=chain_out.at[way, spot, p], dst_ref=chain_in.at[way, spot, p],
            send_sem=chain_send.at[way, spot, p], recv_sem=chain_recv.at[way, spot, p],
            device_id=(my_row + 2 - 4 * way, my_col), device_id_type=MESH,
        )

    def local_sum(spot, p):
        first = (2 * spot + core) * pairs_per
        own = jnp.concatenate([acc[p, first + j] for j in range(pairs_per)], axis=1)
        return own + pair_in[p, spot].astype(F32)

    def hop(way, d, p, edge):
        spot = (1 - way) * (chips - 1 - d) + way * d
        ahead = (1 - 2 * way) * (spot - place)
        behind = (1 - way) * place + way * (chips - 1 - place)
        if edge:
            @pl.when((ahead > 0) & (behind == 0))
            def _():
                chain_out[way, spot, p] = local_sum(spot, p).astype(BF16)
                chain_copy(way, spot, p).start()
        else:
            @pl.when((ahead > 0) & (behind > 0))
            def _():
                chain_copy(way, spot, p).wait_recv()
                total = local_sum(spot, p) + chain_in[way, spot, p].astype(F32)
                chain_out[way, spot, p] = total.astype(BF16)
                chain_copy(way, spot, p).start()

    def edge_hops(p):
        pair_wait(p)
        for d in range(chips - 1):
            hop(0, d, p, True)
            hop(1, d, p, True)

    def middle_hops(p, beside):
        for d in range(chips - 1):
            hop(way, d, p, False)
            if d == 0:
                beside()
            hop(1 - way, d, p, False)

    def deliver(p):
        first = (2 * place + core) * pairs_per
        acc_at = [acc.at[p, first + j] for j in range(pairs_per)]
        for j in range(pairs_per):
            acc_at[j][...] += pair_in[p, place, :, pl.ds(j * PAIR, PAIR)].astype(F32)

        @pl.when(place > 0)
        def _():
            chain_copy(0, place, p).wait_recv()
            for j in range(pairs_per):
                acc_at[j][...] += chain_in[0, place, p, :, pl.ds(j * PAIR, PAIR)].astype(F32)

        @pl.when(place < chips - 1)
        def _():
            chain_copy(1, place, p).wait_recv()
            for j in range(pairs_per):
                acc_at[j][...] += chain_in[1, place, p, :, pl.ds(j * PAIR, PAIR)].astype(F32)

        rows_p = pl.ds(p * part, part)
        for j in range(pairs_per):
            span = pl.ds(j * PAIR, PAIR)
            out_ref[span, rows_p] = jnp.where(mask_buf[rows_p, span] > 0.5, acc_at[j][...], 0.0).T.astype(BF16)

    add_source(0, 0)
    for k in range(1, cols):
        hid_copy(k, 0).wait_send()
    for k in range(1, cols):
        hid_copy(k, 1).start()
    weight_one()
    for k in range(1, cols - 1):
        add_source(k, 0)
    finish(0)
    add_source(0, 1)
    edge_hops(0)
    for k in range(1, cols - 1):
        add_source(k, 1)
    finish(1)
    weight_two()
    edge_hops(1)
    middle_hops(0, weight_three)
    middle_hops(1, weight_four)
    for p in range(PARTS):
        deliver(p)
    weight_end()
    for k in range(1, cols):
        hid_copy(k, 1).wait_send()
    for spot in range(chips):
        for p in range(PARTS):
            pair_copy(spot, p).wait_send()

            @pl.when(spot > place)
            def _():
                chain_copy(0, spot, p).wait_send()

            @pl.when(spot < place)
            def _():
                chain_copy(1, spot, p).wait_send()


def shards(out_grad, out_bits, agg_saved, weight, tiles, tile_coords, tile_count, in_bits):
    rows = lax.axis_size("row")
    cols = lax.axis_size("col")
    nodes, features = out_grad.shape
    scale = 1.0 / math.sqrt(nodes * rows * cols)
    slots = tiles.shape[2]
    row_tiles = cols * nodes // TILE
    col_tiles = rows * nodes // TILE
    chips = rows // 2
    part = features // PARTS
    vmem = pl.BlockSpec(memory_space=pltpu.VMEM)
    hbm = pl.BlockSpec(memory_space=pltpu.HBM)

    dma = pltpu.SemaphoreType.DMA
    band = features // cols
    strip = band // min(rows, band // 8)
    prev_grad, weight_grad = pl.pallas_call(
        functools.partial(exchange, rows, cols, scale),
        out_shape=(
            jax.ShapeDtypeStruct((nodes, features), BF16),
            jax.ShapeDtypeStruct((features, features), F32),
        ),
        in_specs=[hbm] * 6 + [pl.BlockSpec(memory_space=pltpu.SMEM), hbm],
        out_specs=(vmem, vmem),
        scratch_shapes=[
            pltpu.VMEM((cols, band, features), F32),
            pltpu.VMEM((band, features), F32),
            pltpu.VMEM((rows, strip, features), F32),
            pltpu.VMEM((strip, features), F32),
            pltpu.VMEM((band, features), F32),
            pltpu.VMEM((features, features), F32),
            dma((cols,)),
            dma((cols,)),
            dma((rows,)),
            dma((rows,)),
            dma((rows,)),
            dma((rows,)),
            dma((cols,)),
            dma((cols,)),
            pltpu.VMEM((nodes, features), BF16),
            pltpu.VMEM((features // 16, nodes), jnp.int32),
            pltpu.VMEM((nodes, features), BF16),
            pltpu.VMEM((features, features), BF16),
            pltpu.VMEM((2, slots), jnp.int32),
            pltpu.VMEM((features // 16, nodes), jnp.int32),
            pltpu.VMEM((1, row_tiles * col_tiles), jnp.int32),
            pltpu.SMEM((1, row_tiles * col_tiles), jnp.int32),
            pltpu.VMEM((PARTS, part, nodes), BF16),
            pltpu.VMEM((features, features), F32),
            dma((7,)),
            pltpu.VMEM((slots + 1, TILE, TILE), BF16),
            pltpu.VMEM((cols, PARTS, part, nodes), BF16),
            pltpu.VMEM((PARTS, col_tiles // 2, part, PAIR), F32),
            pltpu.VMEM((PARTS, chips, part, nodes), BF16),
            pltpu.VMEM((PARTS, chips, part, nodes), BF16),
            pltpu.VMEM((2, chips, PARTS, part, nodes), BF16),
            pltpu.VMEM((2, chips, PARTS, part, nodes), BF16),
            pltpu.VMEM((features, nodes), F32),
            dma((8,)),
            dma((cols, PARTS)),
            dma((cols, PARTS)),
            dma((PARTS, chips)),
            dma((PARTS, chips)),
            dma((2, chips, PARTS)),
            dma((2, chips, PARTS)),
        ],
        compiler_params=pltpu.CompilerParams(
            collective_id=0, has_side_effects=True, vmem_limit_bytes=56 * 2**20
        ),
        cost_estimate=pl.CostEstimate(
            flops=2 * row_tiles * col_tiles * TILE * TILE * features,
            bytes_accessed=slots * TILE * TILE * 2, transcendentals=0,
        ),
        name="exchange",
    )(out_grad, out_bits.T, agg_saved, weight, tiles[0, 0], tile_coords[0, 0].T, tile_count, in_bits.T)
    return weight_grad, prev_grad


def solution(mesh):
    return jax.shard_map(
        shards,
        mesh=mesh,
        in_specs=(
            P(("row", "col"), None),
            P(("row", "col"), None),
            P(("row", "col"), None),
            P(),
            P("row", "col", None, None, None),
            P("row", "col", None, None),
            P("row", "col"),
            P(("row", "col"), None),
        ),
        out_specs=(P(), P(("row", "col"), None)),
        check_vma=False,
    )
```

time: 68.3 us -> 58.4 us (0.86)
  local copies, waits for them, and re-layouts: 10 us -> 3.34 us
  other arithmetic: 1.58 us -> 0 us
  Pallas kernels: 54.9 us -> 53.6 us
    unnamed x14 -> x2, local copies, waits for them, and re-layouts: 10 us -> 3.34 us
    pallas_call x2 -> x1, Pallas kernels: 54.9 us -> 53.6 us  [shards(): pl.pallas_call(functools.partial(exchange, rows, cols, scale), out_shape=...]
    reduce_min x1 -> x0, other arithmetic: 0.8 us -> none  [shards(): table = jnp.min(jnp.where(hit, slot[:, None], slots), axis=0)]
    add x1 -> x0, other arithmetic: 0.77 us -> none  [shards(): spot = tile_coords[0, 0, :, 0] * col_tiles + tile_coords[0, 0, :, 1]]
where the time goes in v2:
time: 58.4 us; the launch traced here: 58.2 us
  Pallas kernels  53.6 us (92%)
  local copies, waits for them, and re-layouts  3.34 us (6%)
  between operations  1.29 us (2%)
    pallas_call x1, Pallas kernels, shards(): pl.pallas_call(functools.partial(exchange, rows, cols, scale), out_shape=...  53.6 us
    unnamed x2, local copies, waits for them, and re-layouts  3.34 us

profile of v2, /device:TPU:0, one launch (start us, length us, event | category | flops | bytes accessed | tf_op | source)
XLA Modules:
  0.0 58.2 jit_solution(11202250663103449368)
XLA Ops:
  1.3 53.6 %exchange.1 = (bf16[512,256]{1,0:T(8,128)(2,1)}, f32[256,256]{1,0:T(8,128)}) custom-call(bf16[512,256]{1,0:T(8,128)(2,1)} %grad_hbm.1, s32[16,512]{1,0:T(8,128)} %bitcast.7, bf16[512,256]{1,0:T(8,128)(2,1)} %agg_hbm.1, bf16[256,256]{1,0:T(8,128)(2,1)} %weight_hbm.1, bf16[512,128,128]{2,1,0:T(8,128)(2,1)} %bitcast.6, s32[2,512]{1,0:T(2,128)} %bitcast.9, ...), custom_call_target="tpu_custom_call" | custom-call | flops 4294967296 | bytes 16777216 | tf_op jit(solution)/shard_map/exchange/pallas_call | solution.py:392
  54.8 1.7 %copy.13 = f32[256,256]{1,0:T(8,128)} copy(f32[256,256]{1,0:T(8,128)} %get-tuple-element.8) | data formatting | bytes 524288
  56.5 1.7 %copy.14 = bf16[512,256]{1,0:T(8,128)(2,1)} copy(bf16[512,256]{1,0:T(8,128)(2,1)} %get-tuple-element.9) | data formatting | bytes 524288

commit v3 on v2

--- a/solution.py
+++ b/solution.py
@@ -111,9 +111,18 @@
     def landed(ref, sem):
         pltpu.make_async_copy(ref, ref, sem).wait()
 
-    for k in range(1, cols):
-        hid_copy(k, 0).start()
-
+    near = range(1, cols - 1)
+    far = range(cols - 1, cols)
+
+    def send(group, p):
+        for k in group:
+            hid_copy(k, p).start()
+
+    def sent(group, p):
+        for k in group:
+            hid_copy(k, p).wait_send()
+
+    send(near, 0)
     gathered[my_col] = hidden_ref[...]
     tile_buf[slots] = jnp.zeros((TILE, TILE), BF16)
     for load in inputs[3:]:
@@ -134,6 +143,8 @@
         agg_buf[...], masked, (((0,), (0,)), ((), ())), preferred_element_type=F32
     )
     mask_buf[...] = bit_mask(inbits_buf[...], features, True).astype(F32)
+    sent(near, 0)
+    send(far, 0)
     to_scalars.wait()
     for load in loads:
         load.wait()
@@ -147,14 +158,17 @@
             )
         return jnp.dot(gathered[source, p], jnp.concatenate(strips, axis=0), preferred_element_type=F32)
 
-    def add_source(k, p):
-        if k:
-            landed(gathered.at[peers[k], p], hid_recv.at[peers[k], p])
-
-        @pl.loop(0, col_tiles // 2)
+    def add_sources(group, p):
+        for k in group:
+            if k:
+                landed(gathered.at[peers[k], p], hid_recv.at[peers[k], p])
+
+        @pl.loop(0, col_tiles // 2, unroll=4)
         def _(pair):
-            value = product(peers[k], pair, p)
-            if k:
+            value = product(peers[group[0]], pair, p)
+            for k in group[1:]:
+                value += product(peers[k], pair, p)
+            if group[0]:
                 value += acc[p, pair]
             acc[p, pair] = value
 
@@ -337,19 +351,17 @@
             span = pl.ds(j * PAIR, PAIR)
             out_ref[span, rows_p] = jnp.where(mask_buf[rows_p, span] > 0.5, acc_at[j][...], 0.0).T.astype(BF16)
 
-    add_source(0, 0)
-    for k in range(1, cols):
-        hid_copy(k, 0).wait_send()
-    for k in range(1, cols):
-        hid_copy(k, 1).start()
+    add_sources([0], 0)
+    sent(far, 0)
+    send(near, 1)
+    add_sources(near, 0)
+    finish(0)
+    sent(near, 1)
+    send(far, 1)
     weight_one()
-    for k in range(1, cols - 1):
-        add_source(k, 0)
-    finish(0)
-    add_source(0, 1)
+    add_sources([0], 1)
     edge_hops(0)
-    for k in range(1, cols - 1):
-        add_source(k, 1)
+    add_sources(near, 1)
     finish(1)
     weight_two()
     edge_hops(1)
@@ -358,8 +370,7 @@
     for p in range(PARTS):
         deliver(p)
     weight_end()
-    for k in range(1, cols):
-        hid_copy(k, 1).wait_send()
+    sent(far, 1)
     for spot in range(chips):
         for p in range(PARTS):
             pair_copy(spot, p).wait_send()
@@ -371,6 +382,18 @@
             @pl.when(spot < place)
             def _():
                 chain_copy(1, spot, p).wait_send()
+
+
+def deliver_all(prev_in, weight_in, prev_out, weight_out, sems):
+    copies = []
+    for i, (src, dst) in enumerate(((prev_in, prev_out), (weight_in, weight_out))):
+        chunk = src.shape[0] // 4
+        for j in range(4):
+            span = pl.ds(j * chunk, chunk)
+            copies.append(pltpu.make_async_copy(src.at[span], dst.at[span], sems.at[i, j]))
+            copies[-1].start()
+    for copy in copies:
+        copy.wait()
 
 
 def shards(out_grad, out_bits, agg_saved, weight, tiles, tile_coords, tile_count, in_bits):
@@ -448,6 +471,19 @@
         ),
         name="exchange",
     )(out_grad, out_bits.T, agg_saved, weight, tiles[0, 0], tile_coords[0, 0].T, tile_count, in_bits.T)
+    hbm_out = pl.BlockSpec(memory_space=pl.ANY)
+    prev_grad, weight_grad = pl.pallas_call(
+        deliver_all,
+        out_shape=(
+            jax.ShapeDtypeStruct((nodes, features), BF16),
+            jax.ShapeDtypeStruct((features, features), F32),
+        ),
+        in_specs=[hbm_out] * 2,
+        out_specs=(hbm_out, hbm_out),
+        scratch_shapes=[dma((2, 4))],
+        compiler_params=pltpu.CompilerParams(vmem_limit_bytes=56 * 2**20),
+        name="deliver",
+    )(prev_grad, weight_grad)
     return weight_grad, prev_grad
 
 

time: 58.4 us -> 66.9 us (1.15)
  Pallas kernels: 53.6 us -> 65.4 us
  local copies, waits for them, and re-layouts: 3.34 us -> 0 us
    pallas_call x0 -> x1, Pallas kernels: none -> 17.1 us  [shards(): pl.pallas_call(deliver_all, out_shape=(jax.ShapeDtypeStruct((nodes, featu...]
    pallas_call x1, Pallas kernels: 53.6 us -> 48.4 us  [shards(): pl.pallas_call(functools.partial(exchange, rows, cols, scale), out_shape=...]
    unnamed x2 -> x0, local copies, waits for them, and re-layouts: 3.34 us -> none
where the time goes in v3:
time: 66.9 us; the launch traced here: 66.7 us
  Pallas kernels  65.4 us (98%)
  between operations  1.29 us (2%)
    pallas_call x1, Pallas kernels, shards(): pl.pallas_call(functools.partial(exchange, rows, cols, scale), out_shape=...  48.4 us
    pallas_call x1, Pallas kernels, shards(): pl.pallas_call(deliver_all, out_shape=(jax.ShapeDtypeStruct((nodes, featu...  17.1 us

profile of v3, /device:TPU:0, one launch (start us, length us, event | category | flops | bytes accessed | tf_op | source)
XLA Modules:
  0.0 66.7 jit_solution(11754624512336714496)
XLA Ops:
  1.3 48.4 %exchange.1 = (bf16[512,256]{1,0:T(8,128)(2,1)}, f32[256,256]{1,0:T(8,128)}) custom-call(bf16[512,256]{1,0:T(8,128)(2,1)} %grad_hbm.1, s32[16,512]{1,0:T(8,128)} %bitcast.7, bf16[512,256]{1,0:T(8,128)(2,1)} %agg_hbm.1, bf16[256,256]{1,0:T(8,128)(2,1)} %weight_hbm.1, bf16[512,128,128]{2,1,0:T(8,128)(2,1)} %bitcast.6, s32[2,512]{1,0:T(2,128)} %bitcast.9, ...), custom_call_target="tpu_custom_call" | custom-call | flops 4294967296 | bytes 16777216 | tf_op jit(solution)/shard_map/exchange/pallas_call | solution.py:415
  49.7 17.1 %deliver.1 = (bf16[512,256]{1,0:T(8,128)(2,1)}, f32[256,256]{1,0:T(8,128)}) custom-call(bf16[512,256]{1,0:T(8,128)(2,1)} %get-tuple-element.6.prev_in, f32[256,256]{1,0:T(8,128)} %get-tuple-element.7.weight_in), custom_call_target="tpu_custom_call" | custom-call | tf_op jit(solution)/shard_map/deliver/pallas_call | solution.py:475

commit v4 on v3

--- a/solution.py
+++ b/solution.py
@@ -123,7 +123,6 @@
             hid_copy(k, p).wait_send()
 
     send(near, 0)
-    gathered[my_col] = hidden_ref[...]
     tile_buf[slots] = jnp.zeros((TILE, TILE), BF16)
     for load in inputs[3:]:
         load.wait()
@@ -149,28 +148,33 @@
     for load in loads:
         load.wait()
 
-    def product(source, pair, p):
+    def product(source, pair, p=None):
         strips = []
         for i in range(row_tiles):
             base = (source * row_tiles + i) * col_tiles + 2 * pair
             strips.append(
                 jnp.concatenate([tile_buf[table_ref[0, base]], tile_buf[table_ref[0, base + 1]]], axis=1)
             )
-        return jnp.dot(gathered[source, p], jnp.concatenate(strips, axis=0), preferred_element_type=F32)
+        left = hidden_ref[...].reshape(features, nodes) if p is None else gathered[source, p]
+        return jnp.dot(left, jnp.concatenate(strips, axis=0), preferred_element_type=F32)
+
+    def own_source():
+        @pl.loop(0, col_tiles // 2, unroll=4)
+        def _(pair):
+            value = product(my_col, pair)
+            for p in range(PARTS):
+                acc[p, pair] = value[p * part:(p + 1) * part]
 
     def add_sources(group, p):
         for k in group:
-            if k:
-                landed(gathered.at[peers[k], p], hid_recv.at[peers[k], p])
+            landed(gathered.at[peers[k], p], hid_recv.at[peers[k], p])
 
         @pl.loop(0, col_tiles // 2, unroll=4)
         def _(pair):
             value = product(peers[group[0]], pair, p)
             for k in group[1:]:
                 value += product(peers[k], pair, p)
-            if group[0]:
-                value += acc[p, pair]
-            acc[p, pair] = value
+            acc[p, pair] += value
 
     band = features // cols
     owners = min(rows, band // 8)
@@ -282,10 +286,6 @@
                 pair = (2 * spot + core) * pairs_per + j
                 acc[p, pair] += product(peers[cols - 1], pair, p)
 
-    def pair_wait(p):
-        for spot in order:
-            pair_copy(spot, p).wait_recv()
-
     def chain_copy(way, spot, p):
         return pltpu.make_async_remote_copy(
             src_ref=chain_out.at[way, spot, p], dst_ref=chain_in.at[way, spot, p],
@@ -305,25 +305,27 @@
         if edge:
             @pl.when((ahead > 0) & (behind == 0))
             def _():
+                pair_copy(spot, p).wait_recv()
                 chain_out[way, spot, p] = local_sum(spot, p).astype(BF16)
                 chain_copy(way, spot, p).start()
         else:
             @pl.when((ahead > 0) & (behind > 0))
             def _():
+                pair_copy(spot, p).wait_recv()
                 chain_copy(way, spot, p).wait_recv()
                 total = local_sum(spot, p) + chain_in[way, spot, p].astype(F32)
                 chain_out[way, spot, p] = total.astype(BF16)
                 chain_copy(way, spot, p).start()
 
     def edge_hops(p):
-        pair_wait(p)
         for d in range(chips - 1):
             hop(0, d, p, True)
             hop(1, d, p, True)
 
     def middle_hops(p, beside):
         for d in range(chips - 1):
-            hop(way, d, p, False)
+            if d or p:
+                hop(way, d, p, False)
             if d == 0:
                 beside()
             hop(1 - way, d, p, False)
@@ -331,6 +333,7 @@
     def deliver(p):
         first = (2 * place + core) * pairs_per
         acc_at = [acc.at[p, first + j] for j in range(pairs_per)]
+        pair_copy(place, p).wait_recv()
         for j in range(pairs_per):
             acc_at[j][...] += pair_in[p, place, :, pl.ds(j * PAIR, PAIR)].astype(F32)
 
@@ -351,17 +354,17 @@
             span = pl.ds(j * PAIR, PAIR)
             out_ref[span, rows_p] = jnp.where(mask_buf[rows_p, span] > 0.5, acc_at[j][...], 0.0).T.astype(BF16)
 
-    add_sources([0], 0)
+    own_source()
     sent(far, 0)
     send(near, 1)
     add_sources(near, 0)
     finish(0)
     sent(near, 1)
     send(far, 1)
+    edge_hops(0)
     weight_one()
-    add_sources([0], 1)
-    edge_hops(0)
     add_sources(near, 1)
+    hop(way, 0, 0, False)
     finish(1)
     weight_two()
     edge_hops(1)
@@ -384,15 +387,20 @@
                 chain_copy(1, spot, p).wait_send()
 
 
-def deliver_all(prev_in, weight_in, prev_out, weight_out, sems):
-    copies = []
-    for i, (src, dst) in enumerate(((prev_in, prev_out), (weight_in, weight_out))):
+def deliver_all(prev_in, weight_in, prev_out, weight_out, prev_buf, weight_buf, sems):
+    inward, outward = [], []
+    for i, (src, buf, dst) in enumerate(((prev_in, prev_buf, prev_out), (weight_in, weight_buf, weight_out))):
         chunk = src.shape[0] // 4
         for j in range(4):
             span = pl.ds(j * chunk, chunk)
-            copies.append(pltpu.make_async_copy(src.at[span], dst.at[span], sems.at[i, j]))
-            copies[-1].start()
-    for copy in copies:
+            inward.append(pltpu.make_async_copy(src.at[span], buf.at[span], sems.at[0, i, j]))
+            outward.append(pltpu.make_async_copy(buf.at[span], dst.at[span], sems.at[1, i, j]))
+    for copy in inward:
+        copy.start()
+    for first, second in zip(inward, outward):
+        first.wait()
+        second.start()
+    for copy in outward:
         copy.wait()
 
 
@@ -480,7 +488,11 @@
         ),
         in_specs=[hbm_out] * 2,
         out_specs=(hbm_out, hbm_out),
-        scratch_shapes=[dma((2, 4))],
+        scratch_shapes=[
+            pltpu.VMEM((nodes, features), BF16),
+            pltpu.VMEM((features, features), F32),
+            dma((2, 2, 4)),
+        ],
         compiler_params=pltpu.CompilerParams(vmem_limit_bytes=56 * 2**20),
         name="deliver",
     )(prev_grad, weight_grad)

time: 66.9 us -> 51.2 us (0.77)
  Pallas kernels: 65.4 us -> 49.7 us
    pallas_call x1, Pallas kernels: 17.1 us -> 1.83 us  [shards(): pl.pallas_call(deliver_all, out_shape=(jax.ShapeDtypeStruct((nodes, featu...]
where the time goes in v4:
time: 51.2 us; the launch traced here: 51 us
  Pallas kernels  49.7 us (97%)
  between operations  1.29 us (3%)
    pallas_call x1, Pallas kernels, shards(): pl.pallas_call(functools.partial(exchange, rows, cols, scale), out_shape=...  47.9 us
    pallas_call x1, Pallas kernels, shards(): pl.pallas_call(deliver_all, out_shape=(jax.ShapeDtypeStruct((nodes, featu...  1.83 us

profile of v4, /device:TPU:0, one launch (start us, length us, event | category | flops | bytes accessed | tf_op | source)
XLA Modules:
  0.0 51.0 jit_solution(8106549195427991443)
XLA Ops:
  1.3 47.9 %exchange.1 = (bf16[512,256]{1,0:T(8,128)(2,1)}, f32[256,256]{1,0:T(8,128)}) custom-call(bf16[512,256]{1,0:T(8,128)(2,1)} %grad_hbm.1, s32[16,512]{1,0:T(8,128)} %bitcast.7, bf16[512,256]{1,0:T(8,128)(2,1)} %agg_hbm.1, bf16[256,256]{1,0:T(8,128)(2,1)} %weight_hbm.1, bf16[512,128,128]{2,1,0:T(8,128)(2,1)} %bitcast.6, s32[2,512]{1,0:T(2,128)} %bitcast.9, ...), custom_call_target="tpu_custom_call" | custom-call | flops 4294967296 | bytes 16777216 | tf_op jit(solution)/shard_map/exchange/pallas_call | solution.py:423
  49.2 1.8 %deliver.1 = (bf16[512,256]{1,0:T(8,128)(2,1)}, f32[256,256]{1,0:T(8,128)}) custom-call(bf16[512,256]{1,0:T(8,128)(2,1)} %get-tuple-element.6.prev_in, f32[256,256]{1,0:T(8,128)} %get-tuple-element.7.weight_in), custom_call_target="tpu_custom_call" | custom-call | tf_op jit(solution)/shard_map/deliver/pallas_call | solution.py:483

commit v5 on v4

--- a/solution.py
+++ b/solution.py
@@ -51,7 +51,7 @@
     out_ref, weight_ref,
     by_col, col_sum, by_row, row_sum, col_total, total_buf,
     w1_send, w1_recv, w2_send, w2_recv, w3_send, w3_recv, w4_send, w4_recv,
-    grad_buf, bits_buf, agg_buf, mat_buf, coords_buf, inbits_buf, table_buf, table_ref, hidden_ref, part_ref, load_sem,
+    grad_buf, bits_buf, agg_buf, mat_buf, coords_buf, inbits_buf, table_buf, table_ref, hidden_ref, part_ref, part_low, load_sem,
     tile_buf, gathered, acc, pair_out, pair_in, chain_out, chain_in, mask_buf,
     tile_sem, hid_send, hid_recv, pair_send, pair_recv, chain_send, chain_recv,
 ):
@@ -141,6 +141,7 @@
     part_ref[...] = scale * lax.dot_general(
         agg_buf[...], masked, (((0,), (0,)), ((), ())), preferred_element_type=F32
     )
+    part_low[...] = part_ref[...].astype(BF16)
     mask_buf[...] = bit_mask(inbits_buf[...], features, True).astype(F32)
     sent(near, 0)
     send(far, 0)
@@ -182,7 +183,7 @@
 
     def w1_copy(k):
         return pltpu.make_async_remote_copy(
-            src_ref=part_ref.at[pl.ds(pl.multiple_of(peers[k] * band, 8), band)], dst_ref=by_col.at[my_col],
+            src_ref=part_low.at[pl.ds(pl.multiple_of(peers[k] * band, 16), band)], dst_ref=by_col.at[my_col],
             send_sem=w1_send.at[k], recv_sem=w1_recv.at[my_col],
             device_id=(my_row, peers[k]), device_id_type=MESH,
         )
@@ -216,7 +217,7 @@
         total = part_ref[pl.ds(pl.multiple_of(my_col * band, 8), band), :]
         for k in range(1, cols):
             landed(by_col.at[peers[k]], w1_recv.at[peers[k]])
-            total += by_col[peers[k]]
+            total += by_col[peers[k]].astype(F32)
         col_sum[...] = total
         for i in range(1, rows):
             @pl.when(mates[i] < owners)
@@ -322,12 +323,10 @@
             hop(0, d, p, True)
             hop(1, d, p, True)
 
-    def middle_hops(p, beside):
+    def middle_hops(p):
         for d in range(chips - 1):
             if d or p:
                 hop(way, d, p, False)
-            if d == 0:
-                beside()
             hop(1 - way, d, p, False)
 
     def deliver(p):
@@ -354,22 +353,24 @@
             span = pl.ds(j * PAIR, PAIR)
             out_ref[span, rows_p] = jnp.where(mask_buf[rows_p, span] > 0.5, acc_at[j][...], 0.0).T.astype(BF16)
 
+    weight_one()
     own_source()
     sent(far, 0)
     send(near, 1)
     add_sources(near, 0)
+    weight_two()
     finish(0)
+    weight_three()
     sent(near, 1)
     send(far, 1)
     edge_hops(0)
-    weight_one()
     add_sources(near, 1)
+    weight_four()
     hop(way, 0, 0, False)
     finish(1)
-    weight_two()
     edge_hops(1)
-    middle_hops(0, weight_three)
-    middle_hops(1, weight_four)
+    middle_hops(0)
+    middle_hops(1)
     for p in range(PARTS):
         deliver(p)
     weight_end()
@@ -429,7 +430,7 @@
         in_specs=[hbm] * 6 + [pl.BlockSpec(memory_space=pltpu.SMEM), hbm],
         out_specs=(vmem, vmem),
         scratch_shapes=[
-            pltpu.VMEM((cols, band, features), F32),
+            pltpu.VMEM((cols, band, features), BF16),
             pltpu.VMEM((band, features), F32),
             pltpu.VMEM((rows, strip, features), F32),
             pltpu.VMEM((strip, features), F32),
@@ -453,6 +454,7 @@
             pltpu.SMEM((1, row_tiles * col_tiles), jnp.int32),
             pltpu.VMEM((PARTS, part, nodes), BF16),
             pltpu.VMEM((features, features), F32),
+            pltpu.VMEM((features, features), BF16),
             dma((7,)),
             pltpu.VMEM((slots + 1, TILE, TILE), BF16),
             pltpu.VMEM((cols, PARTS, part, nodes), BF16),

time: 51.2 us -> 50.2 us (0.980)
  Pallas kernels: 49.7 us -> 48.7 us
    pallas_call x1, Pallas kernels: 47.9 us -> 46.9 us  [shards(): pl.pallas_call(functools.partial(exchange, rows, cols, scale), out_shape=...]
where the time goes in v5:
time: 50.2 us; the launch traced here: 50 us
  Pallas kernels  48.7 us (97%)
  between operations  1.29 us (3%)
    pallas_call x1, Pallas kernels, shards(): pl.pallas_call(functools.partial(exchange, rows, cols, scale), out_shape=...  46.9 us
    pallas_call x1, Pallas kernels, shards(): pl.pallas_call(deliver_all, out_shape=(jax.ShapeDtypeStruct((nodes, featu...  1.83 us

profile of v5, /device:TPU:0, one launch (start us, length us, event | category | flops | bytes accessed | tf_op | source)
XLA Modules:
  0.0 50.0 jit_solution(18082792879207479425)
XLA Ops:
  1.3 46.9 %exchange.1 = (bf16[512,256]{1,0:T(8,128)(2,1)}, f32[256,256]{1,0:T(8,128)}) custom-call(bf16[512,256]{1,0:T(8,128)(2,1)} %grad_hbm.1, s32[16,512]{1,0:T(8,128)} %bitcast.7, bf16[512,256]{1,0:T(8,128)(2,1)} %agg_hbm.1, bf16[256,256]{1,0:T(8,128)(2,1)} %weight_hbm.1, bf16[512,128,128]{2,1,0:T(8,128)(2,1)} %bitcast.6, s32[2,512]{1,0:T(2,128)} %bitcast.9, ...), custom_call_target="tpu_custom_call" | custom-call | flops 4294967296 | bytes 16777216 | tf_op jit(solution)/shard_map/exchange/pallas_call | solution.py:424
  48.2 1.8 %deliver.1 = (bf16[512,256]{1,0:T(8,128)(2,1)}, f32[256,256]{1,0:T(8,128)}) custom-call(bf16[512,256]{1,0:T(8,128)(2,1)} %get-tuple-element.6.prev_in, f32[256,256]{1,0:T(8,128)} %get-tuple-element.7.weight_in), custom_call_target="tpu_custom_call" | custom-call | tf_op jit(solution)/shard_map/deliver/pallas_call | solution.py:485

commit v6 on v5

--- a/solution.py
+++ b/solution.py
@@ -282,7 +282,6 @@
                 value = acc[p, pair] + product(peers[cols - 1], pair, p)
                 pair_out[p, spot, :, pl.ds(j * PAIR, PAIR)] = value.astype(BF16)
             pair_copy(spot, p).start()
-        for spot in order:
             for j in range(pairs_per):
                 pair = (2 * spot + core) * pairs_per + j
                 acc[p, pair] += product(peers[cols - 1], pair, p)
@@ -358,18 +357,18 @@
     sent(far, 0)
     send(near, 1)
     add_sources(near, 0)
-    weight_two()
     finish(0)
-    weight_three()
     sent(near, 1)
     send(far, 1)
+    weight_two()
     edge_hops(0)
     add_sources(near, 1)
-    weight_four()
+    weight_three()
     hop(way, 0, 0, False)
     finish(1)
     edge_hops(1)
     middle_hops(0)
+    weight_four()
     middle_hops(1)
     for p in range(PARTS):
         deliver(p)

time: 50.2 us -> 49.6 us (0.988)
  Pallas kernels: 48.7 us -> 48.1 us
    pallas_call x1, Pallas kernels: 46.9 us -> 46.3 us  [shards(): pl.pallas_call(functools.partial(exchange, rows, cols, scale), out_shape=...]
where the time goes in v6:
time: 49.6 us; the launch traced here: 49.4 us
  Pallas kernels  48.1 us (97%)
  between operations  1.29 us (3%)
    pallas_call x1, Pallas kernels, shards(): pl.pallas_call(functools.partial(exchange, rows, cols, scale), out_shape=...  46.3 us
    pallas_call x1, Pallas kernels, shards(): pl.pallas_call(deliver_all, out_shape=(jax.ShapeDtypeStruct((nodes, featu...  1.83 us

profile of v6, /device:TPU:0, one launch (start us, length us, event | category | flops | bytes accessed | tf_op | source)
XLA Modules:
  0.0 49.4 jit_solution(5154614670620109280)
XLA Ops:
  1.3 46.3 %exchange.1 = (bf16[512,256]{1,0:T(8,128)(2,1)}, f32[256,256]{1,0:T(8,128)}) custom-call(bf16[512,256]{1,0:T(8,128)(2,1)} %grad_hbm.1, s32[16,512]{1,0:T(8,128)} %bitcast.7, bf16[512,256]{1,0:T(8,128)(2,1)} %agg_hbm.1, bf16[256,256]{1,0:T(8,128)(2,1)} %weight_hbm.1, bf16[512,128,128]{2,1,0:T(8,128)(2,1)} %bitcast.6, s32[2,512]{1,0:T(2,128)} %bitcast.9, ...), custom_call_target="tpu_custom_call" | custom-call | flops 4294967296 | bytes 16777216 | tf_op jit(solution)/shard_map/exchange/pallas_call | solution.py:423
  47.5 1.8 %deliver.1 = (bf16[512,256]{1,0:T(8,128)(2,1)}, f32[256,256]{1,0:T(8,128)}) custom-call(bf16[512,256]{1,0:T(8,128)(2,1)} %get-tuple-element.6.prev_in, f32[256,256]{1,0:T(8,128)} %get-tuple-element.7.weight_in), custom_call_target="tpu_custom_call" | custom-call | tf_op jit(solution)/shard_map/deliver/pallas_call | solution.py:484
